TPU v7x, 256 devices: a whole 4x4x8 slice. The times are simulated.
256 devices in a mesh: wide: 32 (over x, z), narrow: 8 (over y, core).
Axes of the slice: x: 4, y: 4, z: 8, core: 2. Of those that a mesh axis runs over, the one named last changes fastest.
Arguments:
- particle_populations: float32 [64, 2048, 128], P('narrow', 'wide'), may hold values from 0.5 to 2
- kinetic_coefficient_list: float32 [128, 64], replicated, may hold values from -0.75 to 0.75
- stoichiometry_table: float32 [64, 128], replicated, may hold values from -0.5 to 0.5
- sampled_event_draws: int32 [2, 128, 2048, 128], P(None, None, ('wide', 'narrow')), may hold values from 0 to 7
- spreading_rates: float32 [64], P('narrow'), may hold values from 0.02 to 0.12
- adjacency_lists: int32 [2048, 4], P('wide'), may hold values from 0 to 2047, as said below
- adjacent_hop_tallies: int32 [2, 2048, 4], P(None, 'wide'), may hold values from 0 to 3
- current_per_molecule: float32 [64], P('narrow'), may hold values from -1 to 1
- target_boundary_node: int32 [2048, 128], P('wide'), may hold values from 0 to 8191
- membrane_storage_factor: float32 [256, 1024], P('wide', 'narrow'), may hold values from 0.05 to 0.5
- prior_voltage: float32 [256, 1024], P('wide', 'narrow'), may hold values from -6 to 6
Outputs:
- amounts_out: float32 [64, 2048, 128], P('narrow', 'wide')
- potential: float32 [256, 1024], P('wide', 'narrow')
Inputs may be any that keep to these rules, and one draw needn't show every extreme that they name: `adjacency_lists`: each entry names a block at most 64 blocks away from its own; a block may name itself, which adds nothing.
All inputs are finite; a program needn't handle non-finite values.
Results may differ from a plain program's by a relative error of at most 0.0003.
Values sent between devices are 32-bit elements; how exact they have to be, the bound alone decides.
A program may use at most 64 MiB of HBM per device.

v0:
```python
import jax
import jax.numpy as jnp
from jax import lax
from jax.sharding import PartitionSpec as P

INTERVAL_NUMBER = 2
ITERS = 3


def with_halo(cells, sides, width):
    for axis, dim in sides:
        count = lax.axis_size(axis)
        ends = count - 1
        head = lax.slice_in_dim(cells, 0, width, axis=dim)
        tail = lax.slice_in_dim(cells, cells.shape[dim] - width, cells.shape[dim], axis=dim)
        cells = jnp.concatenate(
            [
                lax.ppermute(tail, axis, [(i, (i + 1) % count) for i in range(ends)]),
                cells,
                lax.ppermute(head, axis, [((i + 1) % count, i) for i in range(ends)]),
            ],
            axis=dim,
        )
    return cells


def cellwise_chemistry_change(
    particle_populations, kinetic_coefficient_list, stoichiometry_table, sampled_event_draws
):
    intensity_of_event = jnp.einsum(
        "cl,lug->cug",
        kinetic_coefficient_list,
        particle_populations,
        precision=lax.Precision.HIGHEST,
    )
    realized_event_tally = intensity_of_event * (
        sampled_event_draws.astype(jnp.float32) * (1.0 / 3.5)
    )
    stoichiometric_shift = jnp.einsum(
        "xk,kdl->xdl", stoichiometry_table, realized_event_tally, precision=lax.Precision.HIGHEST
    )
    return particle_populations + 0.25 * stoichiometric_shift


def broaden_groups(
    particle_populations, kinetic_coefficient_list, stoichiometry_table, sampled_event_draws
):
    gathered_entries = lax.all_to_all(
        particle_populations, "narrow", split_axis=1, concat_axis=0, tiled=True
    )
    refreshed_configuration = cellwise_chemistry_change(
        gathered_entries, kinetic_coefficient_list, stoichiometry_table, sampled_event_draws
    )
    reacted_species = lax.all_to_all(
        refreshed_configuration, "narrow", split_axis=0, concat_axis=1, tiled=True
    )
    blocks_here = reacted_species.shape[1]
    widened_blocks = with_halo(reacted_species, (("wide", 1),), blocks_here)
    return (reacted_species, widened_blocks)


def diffuse(
    particle_populations, widened_blocks, spreading_rates, local_neighbours, adjacent_hop_tallies
):
    weights = adjacent_hop_tallies.astype(jnp.float32) * 0.5
    flux_sum = jnp.zeros_like(particle_populations)
    for slot_index in range(local_neighbours.shape[1]):
        picked = jnp.take(widened_blocks, local_neighbours[:, slot_index], axis=1)
        flux_sum = flux_sum + weights[:, slot_index][None, :, None] * (
            picked - particle_populations
        )
    return particle_populations + spreading_rates[:, None, None] * flux_sum


def membrane(field, membrane_storage_factor):
    padded = with_halo(field, (("wide", 0), ("narrow", 1)), 1)
    beside_all = padded[2:, 1:-1] + padded[:-2, 1:-1] + padded[1:-1, 2:] + padded[1:-1, :-2]
    return (4.0 + membrane_storage_factor) * field - beside_all


def squares(residual):
    return lax.psum(jnp.sum(residual * residual), ("wide", "narrow"))


def shards(
    particle_populations,
    kinetic_coefficient_list,
    stoichiometry_table,
    sampled_event_draws,
    spreading_rates,
    adjacency_lists,
    adjacent_hop_tallies,
    current_per_molecule,
    target_boundary_node,
    membrane_storage_factor,
    prior_voltage,
):
    blocks_here = particle_populations.shape[1]
    first_block = lax.axis_index("wide") * blocks_here - blocks_here
    local_neighbours = adjacency_lists - first_block
    for poisson_interval_progress in range(INTERVAL_NUMBER):
        reacted_species, widened_blocks = broaden_groups(
            particle_populations,
            kinetic_coefficient_list,
            stoichiometry_table,
            sampled_event_draws[poisson_interval_progress],
        )
        particle_populations = diffuse(
            reacted_species,
            widened_blocks,
            spreading_rates,
            local_neighbours,
            adjacent_hop_tallies[poisson_interval_progress],
        )
    current = jnp.einsum(
        "s,sbt->bt", current_per_molecule, particle_populations, precision=lax.Precision.HIGHEST
    )
    rows_here, cols_here = membrane_storage_factor.shape
    cols_wide = cols_here * lax.axis_size("narrow")
    vertex_sums = jax.ops.segment_sum(
        current.reshape(-1), target_boundary_node.reshape(-1), num_segments=rows_here * cols_wide
    )
    source = lax.psum_scatter(
        vertex_sums.reshape(rows_here, cols_wide), "narrow", scatter_dimension=1, tiled=True
    )
    right_side = membrane_storage_factor * prior_voltage + source
    potential = jnp.zeros_like(right_side)
    residual = right_side
    direction = right_side
    norm_now = squares(residual)
    for iteration in range(ITERS):
        applied = membrane(direction, membrane_storage_factor)
        step_size = norm_now / lax.psum(jnp.sum(direction * applied), ("wide", "narrow"))
        potential = potential + step_size * direction
        residual = residual - step_size * applied
        norm_next = squares(residual)
        direction = residual + norm_next / norm_now * direction
        norm_now = norm_next
    return (particle_populations, potential)


def solution(mesh):
    return jax.shard_map(
        shards,
        mesh=mesh,
        in_specs=(
            P("narrow", "wide", None),
            P(),
            P(),
            P(None, None, ("wide", "narrow"), None),
            P("narrow"),
            P("wide", None),
            P(None, "wide", None),
            P("narrow"),
            P("wide", None),
            P("wide", "narrow"),
            P("wide", "narrow"),
        ),
        out_specs=(P("narrow", "wide", None), P("wide", "narrow")),
        check_vma=False,
    )
```

profile of v0, /device:TPU:1, one launch (start us, length us, event | category | flops | bytes accessed | tf_op | source)
XLA Modules:
  0.0 611.1 jit_solution(5932470024730925285)
XLA Ops:
  9.1 6.6 %all-to-all-start = ((f32[8,64,128]{2,0,1:T(8,128)}), f32[8,64,128]{2,0,1:T(8,128)S(1)}, u32[]{:S(2)}, u32[]{:S(2)}) async-start(f32[8,64,128]{2,0,1:T(8,128)} %copy.26), calls=%async_computation | async-start | bytes 524288 | tf_op jit(solution)/shard_map/all_to_all | solution.py:48
  16.4 5.7 all-to-all-done
  24.2 4.4 all-to-all-start.1
  29.3 5.8 all-to-all-done.1
  36.4 4.0 collective-permute-start
  40.5 3.3 collective-permute-done.1
  48.8 11.1 %all_to_all.72 = f32[8,64,128]{2,0,1:T(8,128)S(1)} all-to-all(f32[8,64,128]{2,0,1:T(8,128)S(1)} %fusion.22), channel_id=1, replica_groups=mesh['wide'=32,'narrow'=8] {'narrow'}, dimensions={1} | all-to-all | bytes 524288 | tf_op jit(solution)/shard_map/all_to_all | solution.py:48
  61.2 9.9 %all_to_all.73 = f32[64,8,128]{2,1,0:T(8,128)S(1)} all-to-all(f32[64,8,128]{2,1,0:T(8,128)S(1)} %copy.34), channel_id=1, replica_groups=mesh['wide'=32,'narrow'=8] {'narrow'}, dimensions={0} | all-to-all | bytes 524288 | tf_op jit(solution)/shard_map/all_to_all | solution.py:54
  72.5 4.8 collective-permute-start.2
  77.3 3.6 collective-permute-done.3
  85.6 43.4 %scatter_custom_fusion = f32[8192]{0:T(1024)S(1)} fusion(s32[8192]{0:T(1024)} %bitcast.174, f32[8192]{0:T(1024)S(1)} %bitcast.173, f32[]{:T(128)} %constant.10.clone.1), kind=kCustom, calls=%fused_computation.60 | custom fusion | flops 8192 | bytes 33280 | tf_op jit(solution)/shard_map/scatter-add | solution.py:120
  129.7 36.1 %reduce-scatter.2.cloned.1.call-done = f32[8,128]{1,0:T(8,128)} async-done(((f32[8,1024]{1,0:T(8,128)}), f32[8,128]{1,0:T(8,128)}) %reduce-scatter.2.cloned.1.call-update) | async-done | bytes 4112 | tf_op jit(solution)/shard_map/reduce_scatter | solution.py:123
  167.7 4.0 collective-permute-start.5
  172.5 4.1 collective-permute-start.7
  176.7 3.2 collective-permute-start.6
  182.3 79.5 %all-reduce = (f32[]{:T(128)}, f32[]{:T(128)}) all-reduce(f32[]{:T(128)} %get-tuple-element.8, f32[]{:T(128)} %get-tuple-element.7), channel_id=1, replica_groups=mesh['wide'=32,'narrow'=8] {'wide','narrow'}, use_global_device_ids=true, to_apply=%region_3.5 | all-reduce | flops 2 | bytes 16 | tf_op jit(solution)/shard_map/psum | solution.py:82
  263.8 74.2 %psum.44 = f32[]{:T(128)} all-reduce(f32[]{:T(128)} %get-tuple-element.13), channel_id=1, replica_groups=mesh['wide'=32,'narrow'=8] {'wide','narrow'}, use_global_device_ids=true, to_apply=%region_7.9 | all-reduce | flops 1 | bytes 8 | tf_op jit(solution)/shard_map/psum | solution.py:82
  340.6 4.0 collective-permute-start.9
  345.4 4.6 collective-permute-start.11
  355.7 76.0 %psum.45 = f32[]{:T(128)} all-reduce(f32[]{:T(128)} %get-tuple-element.11), channel_id=1, replica_groups=mesh['wide'=32,'narrow'=8] {'wide','narrow'}, use_global_device_ids=true, to_apply=%region_9.11 | all-reduce | flops 1 | bytes 8 | tf_op jit(solution)/shard_map/psum | solution.py:133
  433.7 74.2 %psum.46 = f32[]{:T(128)} all-reduce(f32[]{:T(128)} %multiply_reduce_fusion), channel_id=1, replica_groups=mesh['wide'=32,'narrow'=8] {'wide','narrow'}, use_global_device_ids=true, to_apply=%region_11.13 | all-reduce | flops 1 | bytes 8 | tf_op jit(solution)/shard_map/psum | solution.py:82
  510.5 4.0 collective-permute-start.13
  515.3 4.6 collective-permute-start.15
  526.3 76.0 %psum.47 = f32[]{:T(128)} all-reduce(f32[]{:T(128)} %fusion.40), channel_id=1, replica_groups=mesh['wide'=32,'narrow'=8] {'wide','narrow'}, use_global_device_ids=true, to_apply=%region_13.15 | all-reduce | flops 1 | bytes 8 | tf_op jit(solution)/shard_map/psum | solution.py:133
  (91 shorter events, 42.8 us)
Async XLA Ops:
  7.2 15.0 %copy-start = (f32[128,64]{0,1:T(8,128)S(1)}, f32[128,64]{0,1:T(8,128)}, u32[]{:S(2)}) copy-start(f32[128,64]{0,1:T(8,128)} %param.14) | copy-start | bytes 98308
  7.2 8.5 %copy-start.1 = (s32[2,128,8,128]{3,2,1,0:T(8,128)S(1)}, s32[2,128,8,128]{3,2,1,0:T(8,128)}, u32[]{:S(2)}) copy-start(s32[2,128,8,128]{3,2,1,0:T(8,128)} %param.16) | copy-start | bytes 3145732
  9.1 13.1 %all-to-all-start = ((f32[8,64,128]{2,0,1:T(8,128)}), f32[8,64,128]{2,0,1:T(8,128)S(1)}, u32[]{:S(2)}, u32[]{:S(2)}) async-start(f32[8,64,128]{2,0,1:T(8,128)} %copy.26), calls=%async_computation | async-start | bytes 524288 | tf_op jit(solution)/shard_map/all_to_all | solution.py:48
  24.2 10.9 %all-to-all-start.1 = ((f32[64,8,128]{2,1,0:T(8,128)}), f32[64,8,128]{2,1,0:T(8,128)S(1)}, u32[]{:S(2)}, u32[]{:S(2)}) async-start(f32[64,8,128]{2,1,0:T(8,128)} %copy.29), calls=%async_computation.1 | async-start | bytes 524288 | tf_op jit(solution)/shard_map/all_to_all | solution.py:54
  28.6 137.2 %reduce-scatter.2.cloned.1.call-start = ((), (), s32[]{:S(2)}) async-start(), calls=%async_computation.5 | async-start | bytes 36864 | tf_op jit(solution)/shard_map/reduce_scatter | solution.py:123
  35.1 8.7 %collective-permute-start.1 = (f32[8,64,128]{2,0,1:T(8,128)S(1)}, f32[8,64,128]{2,0,1:T(8,128)S(1)}, u32[]{:S(2)}, u32[]{:S(2)}) collective-permute-start(f32[8,64,128]{2,0,1:T(8,128)S(1)} %bitcast.166), channel_id=1, source_target_pairs={{8,0},{16,8},{24,16},{32,24},{40,32},{48,40},{56,48},{64,56},{72,6... | collective-permute-start | bytes 786440 | tf_op jit(solution)/shard_map/ppermute | solution.py:20
  36.4 8.3 %collective-permute-start = (f32[8,64,128]{2,0,1:T(8,128)S(1)}, f32[8,64,128]{2,0,1:T(8,128)S(1)}, u32[]{:S(2)}, u32[]{:S(2)}) collective-permute-start(f32[8,64,128]{2,0,1:T(8,128)S(1)} %bitcast.167), channel_id=1, source_target_pairs={{0,8},{8,16},{16,24},{24,32},{32,40},{40,48},{48,56},{56,64},{64,7... | collective-permute-start | bytes 786440 | tf_op jit(solution)/shard_map/ppermute | solution.py:18
  71.2 9.7 %collective-permute-start.3 = (f32[8,64,128]{2,0,1:T(8,128)S(1)}, f32[8,64,128]{2,0,1:T(8,128)S(1)}, u32[]{:S(2)}, u32[]{:S(2)}) collective-permute-start(f32[8,64,128]{2,0,1:T(8,128)S(1)} %bitcast.163), channel_id=1, source_target_pairs={{8,0},{16,8},{24,16},{32,24},{40,32},{48,40},{56,48},{64,56},{72,6... | collective-permute-start | bytes 786440 | tf_op jit(solution)/shard_map/ppermute | solution.py:20
  72.5 9.3 %collective-permute-start.2 = (f32[8,64,128]{2,0,1:T(8,128)S(1)}, f32[8,64,128]{2,0,1:T(8,128)S(1)}, u32[]{:S(2)}, u32[]{:S(2)}) collective-permute-start(f32[8,64,128]{2,0,1:T(8,128)S(1)} %bitcast.164), channel_id=1, source_target_pairs={{0,8},{8,16},{16,24},{24,32},{32,40},{40,48},{48,56},{56,64},{64,7... | collective-permute-start | bytes 786440 | tf_op jit(solution)/shard_map/ppermute | solution.py:18
  84.4 0.9 copy-start.8
  129.6 36.1 %copy-start.3 = (f32[8,128]{1,0:T(8,128)S(1)}, f32[8,128]{1,0:T(8,128)}, u32[]{:S(2)}) copy-start(f32[8,128]{1,0:T(8,128)} %param.22) | copy-start | bytes 12292
  129.6 36.1 %copy-start.5 = (f32[8,128]{1,0:T(8,128)S(1)}, f32[8,128]{1,0:T(8,128)}, u32[]{:S(2)}) copy-start(f32[8,128]{1,0:T(8,128)} %param.23) | copy-start | bytes 12292
  166.5 5.3 collective-permute-start.4
  167.7 4.7 collective-permute-start.5
  172.5 7.3 %collective-permute-start.7 = (f32[10,1]{1,0:T(8,128)S(1)}, f32[10,1]{1,0:T(8,128)S(1)}, u32[]{:S(2)}, u32[]{:S(2)}) collective-permute-start(f32[10,1]{1,0:T(8,128)S(1)} %get-tuple-element.31), channel_id=1, source_target_pairs={{0,1},{1,2},{2,3},{3,4},{4,5},{5,6},{6,7},{8,9},{9,10},{10,11},{11... | collective-permute-start | bytes 128 | tf_op jit(solution)/shard_map/ppermute | solution.py:18
  176.7 5.0 collective-permute-start.6
  339.3 5.3 collective-permute-start.8
  340.6 4.7 collective-permute-start.9
  345.4 6.6 %collective-permute-start.11 = (f32[10,1]{1,0:T(8,128)S(1)}, f32[10,1]{1,0:T(8,128)S(1)}, u32[]{:S(2)}, u32[]{:S(2)}) collective-permute-start(f32[10,1]{1,0:T(8,128)S(1)} %get-tuple-element.29), channel_id=1, source_target_pairs={{0,1},{1,2},{2,3},{3,4},{4,5},{5,6},{6,7},{8,9},{9,10},{10,11},{11... | collective-permute-start | bytes 128 | tf_op jit(solution)/shard_map/ppermute | solution.py:18
  350.0 5.0 collective-permute-start.10
  509.2 5.3 collective-permute-start.12
  510.5 4.7 collective-permute-start.13
  515.3 6.6 %collective-permute-start.15 = (f32[10,1]{1,0:T(8,128)S(1)}, f32[10,1]{1,0:T(8,128)S(1)}, u32[]{:S(2)}, u32[]{:S(2)}) collective-permute-start(f32[10,1]{1,0:T(8,128)S(1)} %get-tuple-element.27), channel_id=1, source_target_pairs={{0,1},{1,2},{2,3},{3,4},{4,5},{5,6},{6,7},{8,9},{9,10},{10,11},{11... | collective-permute-start | bytes 128 | tf_op jit(solution)/shard_map/ppermute | solution.py:18
  519.9 5.0 collective-permute-start.14
  (4 other events, 2.8 us)
Sparse Core Ops, SparseCore 0:
  129.8 35.9 reduce-scatter.1
where the time goes:
time: 613 us; the launch traced here: 611 us
  blocking collectives  401 us (65%)
  waiting for transfers between devices  66.4 us (11%)
  starting transfers between devices  58.4 us (10%)
  other arithmetic  49.7 us (8%)
  between operations  21.1 us (3%)
  local copies, waits for them, and re-layouts  11.9 us (2%)
    psum x3, blocking collectives, squares(): return lax.psum(jnp.sum(residual * residual), ('wide', 'narrow'))  228 us
    psum x2, blocking collectives, shards(): lax.psum(jnp.sum(direction * applied), ('wide', 'narrow'))  152 us
    scatter-add x1, other arithmetic, shards(): jax.ops.segment_sum(current.reshape(-1), target_boundary_node.reshape(-1)...  43.4 us
    reduce_scatter x1, waiting for transfers between devices, shards(): lax.psum_scatter(vertex_sums.reshape(rows_here, cols_wide), 'narrow', sca...  36.1 us
    ppermute x8, starting transfers between devices, with_halo(): lax.ppermute(tail, axis, [(i, (i + 1) % count) for i in range(ends)])  34.1 us
    ppermute x8, waiting for transfers between devices, with_halo(): lax.ppermute(head, axis, [((i + 1) % count, i) for i in range(ends)])  14.8 us
    ppermute x8, starting transfers between devices, with_halo(): lax.ppermute(head, axis, [((i + 1) % count, i) for i in range(ends)])  13.4 us
  transfers between devices with their start and end apart: 19, of which 13 were waited for; matrix products, arithmetic and copies ran while one was open for 0% of the time, Pallas kernels for 0%

commit v1 on v0

v1 whole, which is shorter than its diff:
```python
import functools

import jax
import jax.numpy as jnp
from jax import lax
from jax.experimental import pallas as pl
from jax.experimental.pallas import tpu as pltpu
from jax.sharding import PartitionSpec as P

MESH = pl.DeviceIdType.MESH
F32 = jnp.float32
BF16 = jnp.bfloat16

PARTNERS = ((1, 0), (3, 0), (1, 1), (3, 1), (2, 0), (2, 1), (0, 1))
DIRECT = ((0, 1), (1, 0), (3, 0), (1, 1), (3, 1))
SHIFT = 4.0


def split(x):
    high = x.astype(BF16)
    return high, (x - high.astype(F32)).astype(BF16)


def dot(a, b):
    return jnp.dot(a, b, preferred_element_type=F32)


def dot_nt(a, b):
    return lax.dot_general(a, b, (((1,), (1,)), ((), ())), preferred_element_type=F32)


def iota(shape, dim):
    return lax.broadcasted_iota(jnp.int32, shape, dim)


def inner(p, q, moments):
    total = None
    for i, pi in enumerate(p):
        for j, qj in enumerate(q):
            term = pi * qj * moments[i + j]
            total = term if total is None else total + term
    return total


def krylov_coefficients(moments):
    one = jnp.ones_like(moments[0])
    direction, residual = [one], [one]
    x = [jnp.zeros_like(one)] * 3
    norm = moments[0]
    for iteration in range(3):
        size = len(direction)
        applied = [SHIFT * d for d in direction] + [jnp.zeros_like(one)]
        for i in range(size):
            applied[i + 1] = applied[i + 1] + direction[i]
        step = norm / inner(direction, applied, moments)
        x = [x[i] + step * direction[i] if i < size else x[i] for i in range(3)]
        if iteration == 2:
            return x
        residual = [
            (residual[i] if i < len(residual) else 0.0) - step * applied[i] for i in range(size + 1)
        ]
        fresh = inner(residual, residual, moments)
        ratio = fresh / norm
        norm = fresh
        direction = [
            residual[i] + ratio * direction[i] if i < size else residual[i] for i in range(size + 1)
        ]


def kernel(
    zs, xs,
    pops, kct, sto, draws, rates, adjt, talt, coef, tgt, msf, prior,
    out_pops, out_pot,
    gath, react, halo, diff, draws_v, kct_v, sto_v, adj_v, tal_v, tgt_v, msf_v, pri_v,
    rate_s, coef_s, ep, msfh, kmat, smat, wmat, lot, him, uv, vh, fields, mz, mx,
    loc, dloc, sa, ra, sh, r2, rh, se, re, su, ru, sg, rg, so,
):
    w, n = lax.axis_index("wide"), lax.axis_index("narrow")
    wides = zs * xs
    left, right = lax.rem(w + wides - 1, wides), lax.rem(w + 1, wides)
    y, core = n // 2, lax.rem(n, 2)
    x, z = w // zs, lax.rem(w, zs)

    def peer(rel):
        return lax.rem(y + rel[0], 4) * 2 + lax.rem(core + rel[1], 2)

    def source(rel):
        return peer(((4 - rel[0]) % 4, rel[1]))

    def eight(i):
        return pl.ds(pl.multiple_of(i * 8, 8), 8)

    def send(src, dst, s, r, to):
        pltpu.make_async_remote_copy(
            src_ref=src, dst_ref=dst, send_sem=s, recv_sem=r, device_id=to, device_id_type=MESH
        ).start()

    def wait(ref, sem):
        pltpu.make_async_copy(ref, ref, sem).wait()

    z_line = [x * zs + lax.rem(z + k, zs) for k in range(1, zs)]
    x_line = [lax.rem(x + k, xs) * zs + z for k in range(1, xs)]

    barrier = pltpu.get_barrier_semaphore()
    greet = [(w, peer(rel)) for rel in PARTNERS]
    for side in (left, right):
        greet += [(side, n)] + [(side, peer(rel)) for rel in PARTNERS]
    greet += [(v, n) for v in z_line + x_line]
    for to in greet:
        pl.semaphore_signal(barrier, inc=1, device_id=to, device_id_type=MESH)

    small = [
        (coef, coef_s), (rates, rate_s), (msf, msf_v), (prior, pri_v), (kct, kct_v), (sto, sto_v),
        (adjt, adj_v), (talt, tal_v), (tgt, tgt_v), (pops.at[:, eight(n), :], gath.at[0, eight(n)]),
    ]
    small = [pltpu.make_async_copy(s, d, loc.at[i]) for i, (s, d) in enumerate(small)]
    for copy in small:
        copy.start()
    for k in range(2):
        for b in range(8):
            pltpu.make_async_copy(draws.at[k, :, b, :], draws_v.at[k, b], dloc.at[k]).start()
    pl.semaphore_wait(barrier, len(greet))

    def exchange(k, src):
        for rel in PARTNERS:
            m = peer(rel)
            send(src.at[:, eight(m), :], gath.at[k, eight(n)], sa.at[k], ra.at[k], (w, m))

    exchange(0, pops)

    for copy in small[:4]:
        copy.wait()
    row = iota((8, 128), 0)
    ca = jnp.zeros((8, 128), F32)
    cb = jnp.zeros((8, 128), F32)
    for i in range(8):
        ca = jnp.where(row == i, coef_s[i], ca)
        cb = jnp.where(row == i, rate_s[i], cb)
    ep[0, n] = ca
    ep[1, n] = ca * cb
    ep[2, n] = msf_v[...]
    ep[3, n] = msf_v[...] * pri_v[...]
    for rel in PARTNERS:
        send(ep.at[:, n], ep.at[:, n], se.at[0], re.at[0], (w, peer(rel)))

    for copy in small[4:9]:
        copy.wait()
    kt_high, kt_low = split(kct_v[...])
    kt = jnp.concatenate([kt_high, kt_low, kt_high, kt_low], axis=0).astype(F32)
    kmat[...] = kt.T.astype(BF16)
    s_high, s_low = split(sto_v[...])
    smat[...] = jnp.concatenate(
        [jnp.concatenate([s_high, s_high], 1), jnp.concatenate([s_low, s_low], 1)], axis=0
    )
    place = iota((256, 128), 0)
    own = iota((256, 128), 1)
    inside = jnp.where(place >= 128, place - 128, place)
    inside = jnp.where(inside >= 64, inside - 64, inside)
    for k in range(2):
        for part in range(2):
            if part == 0:
                named = inside + jnp.where(place < 128, 64, 0)
            else:
                named = inside + 128
            table = jnp.zeros((256, 128), F32)
            for j in range(4):
                pad = jnp.zeros((1, 64), jnp.int32)
                near = jnp.concatenate([adj_v[j : j + 1, :] - (w * 64 - 64), pad], axis=1)
                tally = jnp.concatenate([tal_v[k, j : j + 1, :], pad], axis=1)
                weight = tally.astype(F32) * 0.5
                table = table + jnp.where(named == near, weight, 0.0)
                if part == 0:
                    table = table - jnp.where(named == own + 64, weight, 0.0)
            wmat[k, part] = table.T[:64].astype(BF16)

    wait(ep.at[:, 0:7], re.at[0])
    send(ep.at[2], msfh.at[1], se.at[1], re.at[1], (left, n))
    send(ep.at[2], msfh.at[0], se.at[2], re.at[2], (right, n))

    def tables(b, carry):
        node = tgt_v[pl.ds(b, 1), :]
        low = lax.rem(node, 128)
        high = lax.rem(node // 128, 8) * 8 + node // 1024
        lot[b] = jnp.where(iota((128, 128), 0) == low, 1.0, 0.0).astype(BF16)
        him[b] = jnp.where(iota((64, 128), 0) == high, 1.0, 0.0).astype(BF16)
        return carry

    lax.fori_loop(0, 64, tables, 0)

    def chemistry(k):
        wait(draws_v.at[k], dloc.at[k])
        populations = gath.at[k].reshape(512, 128)
        reacted = react.at[k].reshape(512, 128)
        for pair in range(4):
            blocks = (2 * pair, 2 * pair + 1)
            p = jnp.concatenate([populations[pl.ds(b, 64, stride=8), :] for b in blocks], axis=1)
            high, low = split(p)
            propensity = dot(kmat[...], jnp.concatenate([high, high, low, low], axis=0))
            d = jnp.concatenate([draws_v[k, b] for b in blocks], axis=1)
            fired = propensity * (d.astype(F32) * (1.0 / 3.5))
            change = dot(smat[...], jnp.concatenate(split(fired), axis=0))
            p = p + 0.25 * (change[:64] + change[64:])
            for i, b in enumerate(blocks):
                reacted[pl.ds(b, 64, stride=8), :] = p[:, 128 * i : 128 * i + 128]

    def chunk(k, side, m):
        return halo.at[k, pl.ds(8 * side, 8), eight(m), :]

    def send_reacted(k):
        for rel in PARTNERS:
            m = peer(rel)
            send(
                react.at[k, eight(m)], chunk(k, 1, n), sh.at[k], r2.at[k, PARTNERS.index(rel)], (w, m)
            )
        for rel in ((0, 0),) + DIRECT:
            m = peer(rel)
            slot = 7 if rel == (0, 0) else PARTNERS.index(rel)
            send(react.at[k, eight(m)], chunk(k, 2, n), sh.at[k], rh.at[k, 1, slot], (left, m))
            send(react.at[k, eight(m)], chunk(k, 0, n), sh.at[k], rh.at[k, 0, slot], (right, m))
        halo[k, 8:16, eight(n), :] = react[k, eight(n)]

    def forward_reacted(k):
        for i, rel in enumerate(PARTNERS):
            if rel in DIRECT:
                continue
            m = source(rel)
            wait(chunk(k, 1, m), r2.at[k, i])
            send(chunk(k, 1, m), chunk(k, 2, m), sh.at[k], rh.at[k, 1, i], (left, n))
            send(chunk(k, 1, m), chunk(k, 0, m), sh.at[k], rh.at[k, 0, i], (right, n))

    def wait_reacted(k):
        for i, rel in enumerate(PARTNERS):
            if rel in DIRECT:
                wait(chunk(k, 1, source(rel)), r2.at[k, i])
        for i, rel in enumerate(PARTNERS + ((0, 0),)):
            for side in (0, 1):
                wait(chunk(k, 2 * side, source(rel)), rh.at[k, side, i])

    def diffuse(k):
        for pair in range(4):
            parts = [
                split(
                    jnp.concatenate(
                        [halo[k, 8 * side + 2 * pair + i] for i in range(2)], axis=1
                    )
                )
                for side in (1, 0, 2)
            ]
            first = jnp.concatenate(parts[0] + parts[1], axis=0)
            second = jnp.concatenate(parts[2], axis=0)
            flux = dot(wmat[k, 0], first) + dot(wmat[k, 1, :, :128], second)
            for i in range(2):
                s = 2 * pair + i
                diff[k, s] = halo[k, 8 + s] + rate_s[s] * flux[:, 128 * i : 128 * i + 128]

    wait(gath.at[0, 0:56], ra.at[0])
    small[9].wait()
    chemistry(0)
    send_reacted(0)
    forward_reacted(0)
    wait_reacted(0)
    diffuse(0)
    exchange(1, diff.at[0])
    gath[1, eight(n)] = diff[0, :, eight(n), :]

    wait(gath.at[1, 0:56], ra.at[1])
    chemistry(1)
    u = jnp.zeros((8, 128), F32)
    v = jnp.zeros((8, 128), F32)
    for s in range(64):
        tile = react[1, s]
        u = u + ep[0, s // 8, s % 8 : s % 8 + 1, :] * tile
        v = v + ep[1, s // 8, s % 8 : s % 8 + 1, :] * tile
    uv[2, eight(n)] = v
    uv[3, eight(n)] = u
    for rel in PARTNERS:
        mine = uv.at[2:4, eight(n), :]
        send(mine, mine, su.at[0], ru.at[0], (w, peer(rel)))
    for rel in PARTNERS + ((0, 0),):
        send(uv.at[2, eight(n)], uv.at[1, eight(n)], su.at[1], ru.at[1], (left, peer(rel)))
        send(uv.at[2, eight(n)], uv.at[0, eight(n)], su.at[1], ru.at[1], (right, peer(rel)))
    send_reacted(1)

    wait(uv.at[2:4, 0:56, :], ru.at[0])
    wait(uv.at[0:2], ru.at[1])
    vs, vl, vr = split(uv[2]), split(uv[0]), split(uv[1])
    current = (
        uv[3]
        + dot(wmat[1, 0], jnp.concatenate(vs + vl, axis=0))
        + dot(wmat[1, 1, :, :128], jnp.concatenate(vr, axis=0))
    )
    c_high, c_low = split(current)
    total = jnp.zeros((128, 128), F32)
    for pair in range(32):
        rows, columns = [], []
        for b in (2 * pair, 2 * pair + 1):
            mask = him[b]
            rows.append(
                jnp.concatenate([mask * c_high[b : b + 1], mask * c_low[b : b + 1]], axis=0)
            )
            columns.append(lot[b])
        total = total + dot_nt(jnp.concatenate(rows, axis=1), jnp.concatenate(columns, axis=1))
    total = total[:64] + total[64:]
    for c in range(8):
        vh[1, c] = ep[3, c] + total[8 * c : 8 * c + 8]
    send(vh.at[1], vh.at[2], sg.at[0], rg.at[0], (left, n))
    send(vh.at[1], vh.at[0], sg.at[1], rg.at[1], (right, n))
    forward_reacted(1)

    wait(msfh.at[0], re.at[1])
    wait(msfh.at[0], re.at[2])
    wait(vh.at[2], rg.at[0])
    wait(vh.at[0], rg.at[1])

    def wide_rows(parts):
        return jnp.concatenate(
            [jnp.concatenate([part[c] for c in range(8)], axis=1) for part in parts], axis=0
        )

    rows24 = iota((24, 1024), 0)
    columns24 = iota((24, 1024), 1)
    outside = ((w == 0) & (rows24 < 8)) | ((w == wides - 1) & (rows24 >= 16))
    factor = wide_rows([msfh.at[0], ep.at[2], msfh.at[1]])
    vector = jnp.where(outside, 0.0, wide_rows([vh.at[0], vh.at[1], vh.at[2]]))
    vectors = [vector]
    for step in range(3):
        beside = pltpu.roll(vector, 1, 0) + pltpu.roll(vector, 23, 0)
        beside = beside + jnp.where(columns24 == 0, 0.0, pltpu.roll(vector, 1, 1))
        beside = beside + jnp.where(columns24 == 1023, 0.0, pltpu.roll(vector, 1023, 1))
        vector = jnp.where(outside, 0.0, ((4.0 - SHIFT) + factor) * vector - beside)
        vectors.append(vector)
    vectors = [v[8:16] for v in vectors]
    for k in range(3):
        for c in range(8):
            fields[k, c] = vectors[k][:, 128 * c : 128 * c + 128]
    sums = []
    for k in range(6):
        product = vectors[k // 2] * vectors[(k + 1) // 2]
        tile = product[:, :128]
        for c in range(1, 8):
            tile = tile + product[:, 128 * c : 128 * c + 128]
        sums.append(jnp.sum(tile, axis=0, keepdims=True))
    mz[z] = jnp.concatenate(sums + [jnp.zeros((2, 128), F32)], axis=0)
    for to in z_line:
        send(mz.at[z], mz.at[z], so.at[0], so.at[1], (to, n))

    wait_reacted(1)
    diffuse(1)
    amounts = pltpu.make_async_copy(diff.at[1], out_pops, loc.at[10])
    amounts.start()

    wait(mz.at[0 : zs - 1], so.at[1])
    mx[x] = jnp.sum(mz[...], axis=0)
    for to in x_line:
        send(mx.at[x], mx.at[x], so.at[2], so.at[3], (to, n))
    wait(mx.at[0 : xs - 1], so.at[3])
    sums = jnp.sum(jnp.sum(mx[...], axis=0), axis=1, keepdims=True)
    a, b, c = krylov_coefficients([sums[k : k + 1] for k in range(6)])
    msf_v[...] = a * fields[0, n] + b * fields[1, n] + c * fields[2, n]
    voltage = pltpu.make_async_copy(msf_v, out_pot, loc.at[11])
    voltage.start()

    for k in range(2):
        wait(gath.at[k, 0:56], sa.at[k])
        wait(halo.at[k, 0:23], sh.at[k])
    wait(ep.at[:, 0:7], se.at[0])
    wait(msfh.at[0], se.at[1])
    wait(msfh.at[0], se.at[2])
    wait(uv.at[2:4, 0:56, :], su.at[0])
    wait(uv.at[0:2], su.at[1])
    wait(vh.at[0], sg.at[0])
    wait(vh.at[0], sg.at[1])
    wait(mz.at[0 : zs - 1], so.at[0])
    wait(mx.at[0 : xs - 1], so.at[2])
    amounts.wait()
    voltage.wait()


def solution(mesh):
    zs = 8
    xs = mesh.shape["wide"] // zs

    def shards(pops, kinetic, sto, draws, rates, adjacency, tallies, coef, target, msf, prior):
        any_spec = pl.BlockSpec(memory_space=pl.ANY)
        dma = pltpu.SemaphoreType.DMA
        vmem = pltpu.VMEM
        return pl.pallas_call(
            functools.partial(kernel, zs, xs),
            out_shape=(
                jax.ShapeDtypeStruct(pops.shape, F32),
                jax.ShapeDtypeStruct(msf.shape, F32),
            ),
            in_specs=[any_spec] * 11,
            out_specs=(any_spec, any_spec),
            scratch_shapes=[
                vmem((2, 64, 8, 128), F32),
                vmem((2, 64, 8, 128), F32),
                vmem((2, 24, 64, 128), F32),
                vmem((2, 8, 64, 128), F32),
                vmem((2, 8, 128, 128), jnp.int32),
                vmem((64, 128), F32),
                vmem((64, 128), F32),
                vmem((4, 64), jnp.int32),
                vmem((2, 4, 64), jnp.int32),
                vmem((64, 128), jnp.int32),
                vmem((8, 128), F32),
                vmem((8, 128), F32),
                pltpu.SMEM((8,), F32),
                pltpu.SMEM((8,), F32),
                vmem((4, 8, 8, 128), F32),
                vmem((2, 8, 8, 128), F32),
                vmem((128, 256), BF16),
                vmem((128, 256), BF16),
                vmem((2, 2, 64, 256), BF16),
                vmem((64, 128, 128), BF16),
                vmem((64, 64, 128), BF16),
                vmem((4, 64, 128), F32),
                vmem((3, 8, 8, 128), F32),
                vmem((3, 8, 8, 128), F32),
                vmem((zs, 8, 128), F32),
                vmem((xs, 8, 128), F32),
                dma((12,)),
                dma((2,)),
                dma((2,)),
                dma((2,)),
                dma((2,)),
                dma((2, 7)),
                dma((2, 2, 8)),
                dma((3,)),
                dma((3,)),
                dma((2,)),
                dma((2,)),
                dma((2,)),
                dma((2,)),
                dma((4,)),
            ],
            compiler_params=pltpu.CompilerParams(
                collective_id=0, has_side_effects=True, vmem_limit_bytes=48 * 1024 * 1024
            ),
        )(
            pops, kinetic.T, sto, draws, rates, adjacency.T, tallies.transpose(0, 2, 1), coef,
            target, msf, prior,
        )

    return jax.shard_map(
        shards,
        mesh=mesh,
        in_specs=(
            P("narrow", "wide", None),
            P(),
            P(),
            P(None, None, ("wide", "narrow"), None),
            P("narrow"),
            P("wide", None),
            P(None, "wide", None),
            P("narrow"),
            P("wide", None),
            P("wide", "narrow"),
            P("wide", "narrow"),
        ),
        out_specs=(P("narrow", "wide", None), P("wide", "narrow")),
        check_vma=False,
    )
```

time: 613 us -> 65.8 us (0.11)
  the two profiles are of different devices: /device:TPU:1 before, /device:TPU:8 now
where the time goes in v1:
time: 65.8 us; the launch traced here: 65.3 us
  Pallas kernels  56.2 us (85%)
  local copies, waits for them, and re-layouts  8.47 us (13%)
  between operations  0.68 us (1%)
    pallas_call x1, Pallas kernels, shards(): pl.pallas_call(functools.partial(kernel, zs, xs), out_shape=(jax.ShapeDty...  56.2 us
    unnamed x24, local copies, waits for them, and re-layouts  8.47 us

profile of v1, /device:TPU:8, one launch (start us, length us, event | category | flops | bytes accessed | tf_op | source)
XLA Modules:
  0.0 65.3 jit_solution(2201482929938372526)
XLA Ops:
  0.6 0.0 copy-start.5
  0.6 0.0 copy-start.9
  0.7 0.0 copy-start.10
  0.7 0.7 %copy-done.5 = s32[2,64,4]{1,2,0:T(4,128)S(1)} copy-done((s32[2,64,4]{1,2,0:T(4,128)S(1)}, s32[2,64,4]{1,2,0:T(4,128)}, u32[]{:S(2)}) %copy-start.5) | copy-done | bytes 2072
  1.3 0.0 copy-done.9
  1.3 0.0 copy-done.10
  1.3 0.0 copy-start
  1.3 1.2 %copy-done = s32[2,128,8,128]{3,2,1,0:T(8,128)S(1)} copy-done((s32[2,128,8,128]{3,2,1,0:T(8,128)S(1)}, s32[2,128,8,128]{3,2,1,0:T(8,128)}, u32[]{:S(2)}) %copy-start) | copy-done | bytes 1048600
  2.6 0.0 copy-start.1
  2.6 0.9 %copy-done.1 = f32[8,64,128]{2,1,0:T(8,128)S(1)} copy-done((f32[8,64,128]{2,1,0:T(8,128)S(1)}, f32[8,64,128]{2,1,0:T(8,128)}, u32[]{:S(2)}) %copy-start.1) | copy-done | bytes 262168
  3.5 0.0 copy-start.2
  3.5 0.8 %copy-done.2 = f32[128,64]{0,1:T(8,128)S(1)} copy-done((f32[128,64]{0,1:T(8,128)S(1)}, f32[128,64]{0,1:T(8,128)}, u32[]{:S(2)}) %copy-start.2) | copy-done | bytes 32792
  4.3 0.0 copy-start.3
  4.3 0.8 %copy-done.3 = f32[64,128]{1,0:T(8,128)S(1)} copy-done((f32[64,128]{1,0:T(8,128)S(1)}, f32[64,128]{1,0:T(8,128)}, u32[]{:S(2)}) %copy-start.3) | copy-done | bytes 32792
  5.0 0.0 copy-start.4
  5.0 0.8 %copy-done.4 = s32[64,128]{1,0:T(8,128)S(1)} copy-done((s32[64,128]{1,0:T(8,128)S(1)}, s32[64,128]{1,0:T(8,128)}, u32[]{:S(2)}) %copy-start.4) | copy-done | bytes 32792
  5.8 0.0 copy-start.6
  5.8 0.7 %copy-done.6 = f32[8,128]{1,0:T(8,128)S(1)} copy-done((f32[8,128]{1,0:T(8,128)S(1)}, f32[8,128]{1,0:T(8,128)}, u32[]{:S(2)}) %copy-start.6) | copy-done | bytes 4120
  6.5 0.0 copy-start.7
  6.5 0.7 %copy-done.7 = f32[8,128]{1,0:T(8,128)S(1)} copy-done((f32[8,128]{1,0:T(8,128)S(1)}, f32[8,128]{1,0:T(8,128)}, u32[]{:S(2)}) %copy-start.7) | copy-done | bytes 4120
  7.2 0.7 %copy-done.8 = s32[64,4]{0,1:T(4,128)S(1)} copy-done((s32[64,4]{0,1:T(4,128)S(1)}, s32[64,4]{0,1:T(4,128)}, u32[]{:S(2)}) %copy-start.8) | copy-done | bytes 1048
  7.8 56.2 %shard_map.122 = (f32[8,64,128]{2,1,0:T(8,128)S(1)}, f32[8,128]{1,0:T(8,128)S(1)}) custom-call(f32[8,64,128]{2,1,0:T(8,128)S(1)} %copy-done.1, f32[64,128]{1,0:T(8,128)S(1)} %bitcast.3, f32[64,128]{1,0:T(8,128)S(1)} %copy-done.3, s32[2,128,8,128]{3,2,1,0:T(8,128)S(1)} %copy-done, f32[8]{0:T(128)S(1)} %copy-done.9, s32[4,64]{1,0:T(4,128)S(1)} %bitcast.5, ...), custom_call_target="tpu_custom_call" | custom-call | tf_op jit(solution)/shard_map/pallas_call | solution.py:387
  64.0 0.7 %copy.15 = f32[8,64,128]{2,1,0:T(8,128)} copy(f32[8,64,128]{2,1,0:T(8,128)S(1)} %get-tuple-element.4) | data formatting | bytes 524288
  64.7 0.6 copy.16
  (1 shorter events, 0.0 us)
Async XLA Ops:
  0.6 0.7 %copy-start.5 = (s32[2,64,4]{1,2,0:T(4,128)S(1)}, s32[2,64,4]{1,2,0:T(4,128)}, u32[]{:S(2)}) copy-start(s32[2,64,4]{1,2,0:T(4,128)} %param.17) | copy-start | bytes 6148
  0.6 0.7 %copy-start.9 = (f32[8]{0:T(128)S(1)}, f32[8]{0:T(128)}, u32[]{:S(2)}) copy-start(f32[8]{0:T(128)} %rates.1) | copy-start | bytes 100
  0.7 0.7 %copy-start.10 = (f32[8]{0:T(128)S(1)}, f32[8]{0:T(128)}, u32[]{:S(2)}) copy-start(f32[8]{0:T(128)} %coef.1) | copy-start | bytes 100
  1.3 1.2 %copy-start = (s32[2,128,8,128]{3,2,1,0:T(8,128)S(1)}, s32[2,128,8,128]{3,2,1,0:T(8,128)}, u32[]{:S(2)}) copy-start(s32[2,128,8,128]{3,2,1,0:T(8,128)} %draws.1) | copy-start | bytes 3145732
  2.6 0.9 %copy-start.1 = (f32[8,64,128]{2,1,0:T(8,128)S(1)}, f32[8,64,128]{2,1,0:T(8,128)}, u32[]{:S(2)}) copy-start(f32[8,64,128]{2,1,0:T(8,128)} %pops.1) | copy-start | bytes 786436
  3.5 0.8 %copy-start.2 = (f32[128,64]{0,1:T(8,128)S(1)}, f32[128,64]{0,1:T(8,128)}, u32[]{:S(2)}) copy-start(f32[128,64]{0,1:T(8,128)} %param.12) | copy-start | bytes 98308
  4.3 0.8 %copy-start.3 = (f32[64,128]{1,0:T(8,128)S(1)}, f32[64,128]{1,0:T(8,128)}, u32[]{:S(2)}) copy-start(f32[64,128]{1,0:T(8,128)} %sto.1) | copy-start | bytes 98308
  5.0 0.8 %copy-start.4 = (s32[64,128]{1,0:T(8,128)S(1)}, s32[64,128]{1,0:T(8,128)}, u32[]{:S(2)}) copy-start(s32[64,128]{1,0:T(8,128)} %tgt.1) | copy-start | bytes 98308
  5.8 0.7 %copy-start.6 = (f32[8,128]{1,0:T(8,128)S(1)}, f32[8,128]{1,0:T(8,128)}, u32[]{:S(2)}) copy-start(f32[8,128]{1,0:T(8,128)} %msf.1) | copy-start | bytes 12292
  6.5 0.7 %copy-start.7 = (f32[8,128]{1,0:T(8,128)S(1)}, f32[8,128]{1,0:T(8,128)}, u32[]{:S(2)}) copy-start(f32[8,128]{1,0:T(8,128)} %prior.1) | copy-start | bytes 12292
  7.2 0.7 %copy-start.8 = (s32[64,4]{0,1:T(4,128)S(1)}, s32[64,4]{0,1:T(4,128)}, u32[]{:S(2)}) copy-start(s32[64,4]{0,1:T(4,128)} %param.16) | copy-start | bytes 3076

commit v2 on v1

--- a/solution.py
+++ b/solution.py
@@ -12,8 +12,10 @@
 BF16 = jnp.bfloat16
 
 PARTNERS = ((1, 0), (3, 0), (1, 1), (3, 1), (2, 0), (2, 1), (0, 1))
-DIRECT = ((0, 1), (1, 0), (3, 0), (1, 1), (3, 1))
+DIRECT = PARTNERS
 SHIFT = 4.0
+VLIM = 62
+HALF = (4, 8)
 
 
 def split(x):
@@ -72,7 +74,7 @@
     pops, kct, sto, draws, rates, adjt, talt, coef, tgt, msf, prior,
     out_pops, out_pot,
     gath, react, halo, diff, draws_v, kct_v, sto_v, adj_v, tal_v, tgt_v, msf_v, pri_v,
-    rate_s, coef_s, ep, msfh, kmat, smat, wmat, lot, him, uv, vh, fields, mz, mx,
+    rate_s, coef_s, ep, msfh, kmat, smat, wmat, lot, him, uv, vh, fields, mz,
     loc, dloc, sa, ra, sh, r2, rh, se, re, su, ru, sg, rg, so,
 ):
     w, n = lax.axis_index("wide"), lax.axis_index("narrow")
@@ -98,14 +100,15 @@
     def wait(ref, sem):
         pltpu.make_async_copy(ref, ref, sem).wait()
 
-    z_line = [x * zs + lax.rem(z + k, zs) for k in range(1, zs)]
-    x_line = [lax.rem(x + k, xs) * zs + z for k in range(1, xs)]
+    steps = [(i, j) for i in range(xs) for j in range(zs)][1:]
+    steps.sort(key=lambda s: -(min(s[0], xs - s[0]) + min(s[1], zs - s[1])))
+    others = [lax.rem(x + i, xs) * zs + lax.rem(z + j, zs) for i, j in steps]
 
     barrier = pltpu.get_barrier_semaphore()
     greet = [(w, peer(rel)) for rel in PARTNERS]
     for side in (left, right):
         greet += [(side, n)] + [(side, peer(rel)) for rel in PARTNERS]
-    greet += [(v, n) for v in z_line + x_line]
+    greet += [(v, n) for v in others]
     for to in greet:
         pl.semaphore_signal(barrier, inc=1, device_id=to, device_id_type=MESH)
 
@@ -121,12 +124,10 @@
             pltpu.make_async_copy(draws.at[k, :, b, :], draws_v.at[k, b], dloc.at[k]).start()
     pl.semaphore_wait(barrier, len(greet))
 
-    def exchange(k, src):
-        for rel in PARTNERS:
-            m = peer(rel)
-            send(src.at[:, eight(m), :], gath.at[k, eight(n)], sa.at[k], ra.at[k], (w, m))
-
-    exchange(0, pops)
+    for rel in PARTNERS:
+        m = peer(rel)
+        send(pops.at[:, eight(m), :], gath.at[0, eight(n)], sa.at[0], ra.at[0], (w, m))
+
 
     for copy in small[:4]:
         copy.wait()
@@ -152,31 +153,6 @@
     smat[...] = jnp.concatenate(
         [jnp.concatenate([s_high, s_high], 1), jnp.concatenate([s_low, s_low], 1)], axis=0
     )
-    place = iota((256, 128), 0)
-    own = iota((256, 128), 1)
-    inside = jnp.where(place >= 128, place - 128, place)
-    inside = jnp.where(inside >= 64, inside - 64, inside)
-    for k in range(2):
-        for part in range(2):
-            if part == 0:
-                named = inside + jnp.where(place < 128, 64, 0)
-            else:
-                named = inside + 128
-            table = jnp.zeros((256, 128), F32)
-            for j in range(4):
-                pad = jnp.zeros((1, 64), jnp.int32)
-                near = jnp.concatenate([adj_v[j : j + 1, :] - (w * 64 - 64), pad], axis=1)
-                tally = jnp.concatenate([tal_v[k, j : j + 1, :], pad], axis=1)
-                weight = tally.astype(F32) * 0.5
-                table = table + jnp.where(named == near, weight, 0.0)
-                if part == 0:
-                    table = table - jnp.where(named == own + 64, weight, 0.0)
-            wmat[k, part] = table.T[:64].astype(BF16)
-
-    wait(ep.at[:, 0:7], re.at[0])
-    send(ep.at[2], msfh.at[1], se.at[1], re.at[1], (left, n))
-    send(ep.at[2], msfh.at[0], se.at[2], re.at[2], (right, n))
-
     def tables(b, carry):
         node = tgt_v[pl.ds(b, 1), :]
         low = lax.rem(node, 128)
@@ -185,7 +161,28 @@
         him[b] = jnp.where(iota((64, 128), 0) == high, 1.0, 0.0).astype(BF16)
         return carry
 
-    lax.fori_loop(0, 64, tables, 0)
+    def hop_tables():
+        place = iota((256, 128), 0)
+        own = iota((256, 128), 1)
+        inside = jnp.where(place >= 128, place - 128, place)
+        inside = jnp.where(inside >= 64, inside - 64, inside)
+        for k in range(2):
+            for part in range(2):
+                if part == 0:
+                    named = inside + jnp.where(place < 128, 64, 0)
+                else:
+                    named = inside + 128
+                table = jnp.zeros((256, 128), F32)
+                for j in range(4):
+                    pad = jnp.zeros((1, 64), jnp.int32)
+                    near = jnp.concatenate([adj_v[j : j + 1, :] - (w * 64 - 64), pad], axis=1)
+                    tally = jnp.concatenate([tal_v[k, j : j + 1, :], pad], axis=1)
+                    weight = tally.astype(F32) * 0.5
+                    table = table + jnp.where(named == near, weight, 0.0)
+                    if part == 0:
+                        table = table - jnp.where(named == own + 64, weight, 0.0)
+                wmat[k, part] = table.T[:64].astype(BF16)
+
 
     def chemistry(k):
         wait(draws_v.at[k], dloc.at[k])
@@ -203,41 +200,44 @@
             for i, b in enumerate(blocks):
                 reacted[pl.ds(b, 64, stride=8), :] = p[:, 128 * i : 128 * i + 128]
 
-    def chunk(k, side, m):
-        return halo.at[k, pl.ds(8 * side, 8), eight(m), :]
-
-    def send_reacted(k):
-        for rel in PARTNERS:
+    def chunk(k, side, m, h):
+        return halo.at[k, pl.ds(8 * side + HALF[k] * h, HALF[k]), eight(m), :]
+
+    def send_reacted(k, h):
+        def reacted(m):
+            return react.at[k, pl.ds(pl.multiple_of(8 * m + HALF[k] * h, HALF[k]), HALF[k])]
+
+        for i, rel in enumerate(PARTNERS):
             m = peer(rel)
-            send(
-                react.at[k, eight(m)], chunk(k, 1, n), sh.at[k], r2.at[k, PARTNERS.index(rel)], (w, m)
-            )
+            send(reacted(m), chunk(k, 1, n, h), sh.at[k], r2.at[k, h, i], (w, m))
         for rel in ((0, 0),) + DIRECT:
             m = peer(rel)
             slot = 7 if rel == (0, 0) else PARTNERS.index(rel)
-            send(react.at[k, eight(m)], chunk(k, 2, n), sh.at[k], rh.at[k, 1, slot], (left, m))
-            send(react.at[k, eight(m)], chunk(k, 0, n), sh.at[k], rh.at[k, 0, slot], (right, m))
+            send(reacted(m), chunk(k, 2, n, h), sh.at[k], rh.at[k, h, 1, slot], (left, m))
+            send(reacted(m), chunk(k, 0, n, h), sh.at[k], rh.at[k, h, 0, slot], (right, m))
+
+    def keep_reacted(k):
         halo[k, 8:16, eight(n), :] = react[k, eight(n)]
 
-    def forward_reacted(k):
+    def forward_reacted(k, h):
         for i, rel in enumerate(PARTNERS):
             if rel in DIRECT:
                 continue
             m = source(rel)
-            wait(chunk(k, 1, m), r2.at[k, i])
-            send(chunk(k, 1, m), chunk(k, 2, m), sh.at[k], rh.at[k, 1, i], (left, n))
-            send(chunk(k, 1, m), chunk(k, 0, m), sh.at[k], rh.at[k, 0, i], (right, n))
-
-    def wait_reacted(k):
+            wait(chunk(k, 1, m, h), r2.at[k, h, i])
+            send(chunk(k, 1, m, h), chunk(k, 2, m, h), sh.at[k], rh.at[k, h, 1, i], (left, n))
+            send(chunk(k, 1, m, h), chunk(k, 0, m, h), sh.at[k], rh.at[k, h, 0, i], (right, n))
+
+    def wait_reacted(k, h):
         for i, rel in enumerate(PARTNERS):
             if rel in DIRECT:
-                wait(chunk(k, 1, source(rel)), r2.at[k, i])
+                wait(chunk(k, 1, source(rel), h), r2.at[k, h, i])
         for i, rel in enumerate(PARTNERS + ((0, 0),)):
             for side in (0, 1):
-                wait(chunk(k, 2 * side, source(rel)), rh.at[k, side, i])
-
-    def diffuse(k):
-        for pair in range(4):
+                wait(chunk(k, 2 * side, source(rel), h), rh.at[k, h, side, i])
+
+    def diffuse(k, h):
+        for pair in range(HALF[k] // 2 * h, HALF[k] // 2 * (h + 1)):
             parts = [
                 split(
                     jnp.concatenate(
@@ -256,12 +256,29 @@
     wait(gath.at[0, 0:56], ra.at[0])
     small[9].wait()
     chemistry(0)
-    send_reacted(0)
-    forward_reacted(0)
-    wait_reacted(0)
-    diffuse(0)
-    exchange(1, diff.at[0])
+    for h in range(8 // HALF[0]):
+        send_reacted(0, h)
+    keep_reacted(0)
+    hop_tables()
+    for h in range(8 // HALF[0]):
+        forward_reacted(0, h)
+    lax.fori_loop(0, 24, tables, 0)
+    for h in range(8 // HALF[0]):
+        wait_reacted(0, h)
+        diffuse(0, h)
+        for rel in PARTNERS:
+            m = peer(rel)
+            send(
+                diff.at[0, pl.ds(HALF[0] * h, HALF[0]), eight(m), :],
+                gath.at[1, pl.ds(pl.multiple_of(8 * n + HALF[0] * h, HALF[0]), HALF[0])],
+                sa.at[1], ra.at[1], (w, m),
+            )
     gath[1, eight(n)] = diff[0, :, eight(n), :]
+    lax.fori_loop(24, 64, tables, 0)
+    wait(ep.at[:, 0:7], re.at[0])
+    send(ep.at[2], msfh.at[1], se.at[1], re.at[1], (left, n))
+    send(ep.at[2], msfh.at[0], se.at[2], re.at[2], (right, n))
+
 
     wait(gath.at[1, 0:56], ra.at[1])
     chemistry(1)
@@ -273,13 +290,14 @@
         v = v + ep[1, s // 8, s % 8 : s % 8 + 1, :] * tile
     uv[2, eight(n)] = v
     uv[3, eight(n)] = u
+    for rel in PARTNERS + ((0, 0),):
+        send(uv.at[2, eight(n)], uv.at[1, eight(n)], su.at[1], ru.at[1], (left, peer(rel)))
+        send(uv.at[2, eight(n)], uv.at[0, eight(n)], su.at[1], ru.at[1], (right, peer(rel)))
     for rel in PARTNERS:
         mine = uv.at[2:4, eight(n), :]
         send(mine, mine, su.at[0], ru.at[0], (w, peer(rel)))
-    for rel in PARTNERS + ((0, 0),):
-        send(uv.at[2, eight(n)], uv.at[1, eight(n)], su.at[1], ru.at[1], (left, peer(rel)))
-        send(uv.at[2, eight(n)], uv.at[0, eight(n)], su.at[1], ru.at[1], (right, peer(rel)))
-    send_reacted(1)
+    send_reacted(1, 0)
+    keep_reacted(1)
 
     wait(uv.at[2:4, 0:56, :], ru.at[0])
     wait(uv.at[0:2], ru.at[1])
@@ -305,7 +323,7 @@
         vh[1, c] = ep[3, c] + total[8 * c : 8 * c + 8]
     send(vh.at[1], vh.at[2], sg.at[0], rg.at[0], (left, n))
     send(vh.at[1], vh.at[0], sg.at[1], rg.at[1], (right, n))
-    forward_reacted(1)
+    forward_reacted(1, 0)
 
     wait(msfh.at[0], re.at[1])
     wait(msfh.at[0], re.at[2])
@@ -340,21 +358,21 @@
         for c in range(1, 8):
             tile = tile + product[:, 128 * c : 128 * c + 128]
         sums.append(jnp.sum(tile, axis=0, keepdims=True))
-    mz[z] = jnp.concatenate(sums + [jnp.zeros((2, 128), F32)], axis=0)
-    for to in z_line:
-        send(mz.at[z], mz.at[z], so.at[0], so.at[1], (to, n))
-
-    wait_reacted(1)
-    diffuse(1)
+    tile = jnp.concatenate(sums + [jnp.zeros((2, 128), F32)], axis=0)
+    tile = jnp.sum(tile, axis=1, keepdims=True)
+    diagonal = iota((8, 128), 0) == iota((8, 128), 1)
+    mz[w] = jnp.sum(jnp.where(diagonal, tile, 0.0), axis=0, keepdims=True)
+    for to in others:
+        send(mz.at[w], mz.at[w], so.at[0], so.at[1], (to, n))
+
+    wait_reacted(1, 0)
+    diffuse(1, 0)
     amounts = pltpu.make_async_copy(diff.at[1], out_pops, loc.at[10])
     amounts.start()
 
-    wait(mz.at[0 : zs - 1], so.at[1])
-    mx[x] = jnp.sum(mz[...], axis=0)
-    for to in x_line:
-        send(mx.at[x], mx.at[x], so.at[2], so.at[3], (to, n))
-    wait(mx.at[0 : xs - 1], so.at[3])
-    sums = jnp.sum(jnp.sum(mx[...], axis=0), axis=1, keepdims=True)
+    wait(mz.at[0 : wides - 1], so.at[1])
+    tile = jnp.sum(mz[...].reshape(wides, 128), axis=0, keepdims=True)
+    sums = jnp.sum(jnp.where(diagonal, tile, 0.0), axis=1, keepdims=True)
     a, b, c = krylov_coefficients([sums[k : k + 1] for k in range(6)])
     msf_v[...] = a * fields[0, n] + b * fields[1, n] + c * fields[2, n]
     voltage = pltpu.make_async_copy(msf_v, out_pot, loc.at[11])
@@ -370,8 +388,7 @@
     wait(uv.at[0:2], su.at[1])
     wait(vh.at[0], sg.at[0])
     wait(vh.at[0], sg.at[1])
-    wait(mz.at[0 : zs - 1], so.at[0])
-    wait(mx.at[0 : xs - 1], so.at[2])
+    wait(mz.at[0 : wides - 1], so.at[0])
     amounts.wait()
     voltage.wait()
 
@@ -382,15 +399,16 @@
 
     def shards(pops, kinetic, sto, draws, rates, adjacency, tallies, coef, target, msf, prior):
         any_spec = pl.BlockSpec(memory_space=pl.ANY)
+        hbm_spec = pl.BlockSpec(memory_space=pltpu.HBM)
         dma = pltpu.SemaphoreType.DMA
         vmem = pltpu.VMEM
         return pl.pallas_call(
             functools.partial(kernel, zs, xs),
             out_shape=(
-                jax.ShapeDtypeStruct(pops.shape, F32),
-                jax.ShapeDtypeStruct(msf.shape, F32),
+                pltpu.VMEM(pops.shape, F32),
+                pltpu.VMEM(msf.shape, F32),
             ),
-            in_specs=[any_spec] * 11,
+            in_specs=[hbm_spec] * 11,
             out_specs=(any_spec, any_spec),
             scratch_shapes=[
                 vmem((2, 64, 8, 128), F32),
@@ -417,25 +435,24 @@
                 vmem((4, 64, 128), F32),
                 vmem((3, 8, 8, 128), F32),
                 vmem((3, 8, 8, 128), F32),
-                vmem((zs, 8, 128), F32),
-                vmem((xs, 8, 128), F32),
+                vmem((zs * xs, 1, 128), F32),
                 dma((12,)),
                 dma((2,)),
                 dma((2,)),
                 dma((2,)),
                 dma((2,)),
-                dma((2, 7)),
-                dma((2, 2, 8)),
+                dma((2, 4, 7)),
+                dma((2, 4, 2, 8)),
                 dma((3,)),
                 dma((3,)),
                 dma((2,)),
                 dma((2,)),
                 dma((2,)),
                 dma((2,)),
-                dma((4,)),
+                dma((2,)),
             ],
             compiler_params=pltpu.CompilerParams(
-                collective_id=0, has_side_effects=True, vmem_limit_bytes=48 * 1024 * 1024
+                collective_id=0, has_side_effects=True, vmem_limit_bytes=VLIM * 1024 * 1024
             ),
         )(
             pops, kinetic.T, sto, draws, rates, adjacency.T, tallies.transpose(0, 2, 1), coef,

time: 65.8 us -> 57 us (0.87)
  the two profiles are of different devices: /device:TPU:8 before, /device:TPU:1 now
where the time goes in v2:
time: 57 us; the launch traced here: 56.9 us
  Pallas kernels  55 us (96%)
  local copies, waits for them, and re-layouts  1.3 us (2%)
  between operations  0.64 us (1%)
    pallas_call x1, Pallas kernels, shards(): pl.pallas_call(functools.partial(kernel, zs, xs), out_shape=(pltpu.VMEM(p...  55 us
    unnamed x2, local copies, waits for them, and re-layouts  1.3 us

profile of v2, /device:TPU:1, one launch (start us, length us, event | category | flops | bytes accessed | tf_op | source)
XLA Modules:
  0.0 56.9 jit_solution(4669005456393090802)
XLA Ops:
  0.6 55.0 %shard_map.122 = (f32[8,64,128]{2,1,0:T(8,128)S(1)}, f32[8,128]{1,0:T(8,128)S(1)}) custom-call(f32[8,64,128]{2,1,0:T(8,128)} %pops.1, f32[64,128]{1,0:T(8,128)} %bitcast.3, f32[64,128]{1,0:T(8,128)} %sto.1, s32[2,128,8,128]{3,2,1,0:T(8,128)} %draws.1, f32[8]{0:T(128)} %rates.1, s32[4,64]{1,0:T(4,128)} %bitcast.5, s32[2,4,64]{2,1,0:T(4,128)} %bitcast.4, ...), custom_call_target="tpu_custom_call" | custom-call | tf_op jit(solution)/shard_map/pallas_call | solution.py:405
  55.6 0.7 %copy.15 = f32[8,64,128]{2,1,0:T(8,128)} copy(f32[8,64,128]{2,1,0:T(8,128)S(1)} %get-tuple-element.2) | data formatting | bytes 524288
  56.3 0.6 %copy.16 = f32[8,128]{1,0:T(8,128)} copy(f32[8,128]{1,0:T(8,128)S(1)} %get-tuple-element.3) | data formatting | bytes 8192

commit v3 on v2

--- a/solution.py
+++ b/solution.py
@@ -12,7 +12,7 @@
 BF16 = jnp.bfloat16
 
 PARTNERS = ((1, 0), (3, 0), (1, 1), (3, 1), (2, 0), (2, 1), (0, 1))
-DIRECT = PARTNERS
+DIRECT = ((0, 1), (1, 0), (3, 0), (1, 1), (3, 1))
 SHIFT = 4.0
 VLIM = 62
 HALF = (4, 8)
@@ -74,8 +74,8 @@
     pops, kct, sto, draws, rates, adjt, talt, coef, tgt, msf, prior,
     out_pops, out_pot,
     gath, react, halo, diff, draws_v, kct_v, sto_v, adj_v, tal_v, tgt_v, msf_v, pri_v,
-    rate_s, coef_s, ep, msfh, kmat, smat, wmat, lot, him, uv, vh, fields, mz,
-    loc, dloc, sa, ra, sh, r2, rh, se, re, su, ru, sg, rg, so,
+    rate_s, coef_s, ep, msfh, kmat, smat, wmat, lot, him, uv, vh, edge, fields, mz,
+    loc, dloc, sa, ra, sh, r2, rh, se, re, su, ru, sg, rg, so, near,
 ):
     w, n = lax.axis_index("wide"), lax.axis_index("narrow")
     wides = zs * xs
@@ -106,9 +106,7 @@
 
     barrier = pltpu.get_barrier_semaphore()
     greet = [(w, peer(rel)) for rel in PARTNERS]
-    for side in (left, right):
-        greet += [(side, n)] + [(side, peer(rel)) for rel in PARTNERS]
-    greet += [(v, n) for v in others]
+    greet += [(left, n), (right, n)]
     for to in greet:
         pl.semaphore_signal(barrier, inc=1, device_id=to, device_id_type=MESH)
 
@@ -128,6 +126,13 @@
         m = peer(rel)
         send(pops.at[:, eight(m), :], gath.at[0, eight(n)], sa.at[0], ra.at[0], (w, m))
 
+
+    def reach(level):
+        far = 2**level
+        for to in (lax.rem(w + far, wides), lax.rem(w + wides - far, wides)):
+            pl.semaphore_signal(near.at[level], inc=1, device_id=(to, n), device_id_type=MESH)
+
+    reach(0)
 
     for copy in small[:4]:
         copy.wait()
@@ -256,12 +261,16 @@
     wait(gath.at[0, 0:56], ra.at[0])
     small[9].wait()
     chemistry(0)
+    pl.semaphore_wait(near.at[0], 2)
+    reach(1)
     for h in range(8 // HALF[0]):
         send_reacted(0, h)
     keep_reacted(0)
     hop_tables()
     for h in range(8 // HALF[0]):
         forward_reacted(0, h)
+    pl.semaphore_wait(near.at[1], 2)
+    reach(2)
     lax.fori_loop(0, 24, tables, 0)
     for h in range(8 // HALF[0]):
         wait_reacted(0, h)
@@ -274,6 +283,8 @@
                 sa.at[1], ra.at[1], (w, m),
             )
     gath[1, eight(n)] = diff[0, :, eight(n), :]
+    pl.semaphore_wait(near.at[2], 2)
+    reach(3)
     lax.fori_loop(24, 64, tables, 0)
     wait(ep.at[:, 0:7], re.at[0])
     send(ep.at[2], msfh.at[1], se.at[1], re.at[1], (left, n))
@@ -298,6 +309,7 @@
         send(mine, mine, su.at[0], ru.at[0], (w, peer(rel)))
     send_reacted(1, 0)
     keep_reacted(1)
+    pl.semaphore_wait(near.at[3], 2)
 
     wait(uv.at[2:4, 0:56, :], ru.at[0])
     wait(uv.at[0:2], ru.at[1])
@@ -321,14 +333,22 @@
     total = total[:64] + total[64:]
     for c in range(8):
         vh[1, c] = ep[3, c] + total[8 * c : 8 * c + 8]
-    send(vh.at[1], vh.at[2], sg.at[0], rg.at[0], (left, n))
-    send(vh.at[1], vh.at[0], sg.at[1], rg.at[1], (right, n))
+    for c in range(4):
+        one, two = vh[1, 2 * c], vh[1, 2 * c + 1]
+        edge[0, c] = jnp.where(row < 3, one, pltpu.roll(two, 3, 0))
+        edge[1, c] = jnp.where(row < 3, pltpu.roll(one, 3, 0), two)
+    send(edge.at[0], edge.at[3], sg.at[0], rg.at[0], (left, n))
+    send(edge.at[1], edge.at[2], sg.at[1], rg.at[1], (right, n))
     forward_reacted(1, 0)
 
     wait(msfh.at[0], re.at[1])
     wait(msfh.at[0], re.at[2])
-    wait(vh.at[2], rg.at[0])
-    wait(vh.at[0], rg.at[1])
+    wait(edge.at[3], rg.at[0])
+    wait(edge.at[2], rg.at[1])
+    for c in range(4):
+        above, below = edge[2, c], edge[3, c]
+        vh[0, 2 * c], vh[0, 2 * c + 1] = pltpu.roll(above, 5, 0), above
+        vh[2, 2 * c], vh[2, 2 * c + 1] = below, pltpu.roll(below, 5, 0)
 
     def wide_rows(parts):
         return jnp.concatenate(
@@ -386,8 +406,8 @@
     wait(msfh.at[0], se.at[2])
     wait(uv.at[2:4, 0:56, :], su.at[0])
     wait(uv.at[0:2], su.at[1])
-    wait(vh.at[0], sg.at[0])
-    wait(vh.at[0], sg.at[1])
+    wait(edge.at[0], sg.at[0])
+    wait(edge.at[1], sg.at[1])
     wait(mz.at[0 : wides - 1], so.at[0])
     amounts.wait()
     voltage.wait()
@@ -434,6 +454,7 @@
                 vmem((64, 64, 128), BF16),
                 vmem((4, 64, 128), F32),
                 vmem((3, 8, 8, 128), F32),
+                vmem((4, 4, 8, 128), F32),
                 vmem((3, 8, 8, 128), F32),
                 vmem((zs * xs, 1, 128), F32),
                 dma((12,)),
@@ -450,6 +471,7 @@
                 dma((2,)),
                 dma((2,)),
                 dma((2,)),
+                pltpu.SemaphoreType.REGULAR((4,)),
             ],
             compiler_params=pltpu.CompilerParams(
                 collective_id=0, has_side_effects=True, vmem_limit_bytes=VLIM * 1024 * 1024

time: 57 us -> 51.1 us (0.90)
  Pallas kernels: 55 us -> 49 us
    pallas_call x1, Pallas kernels: 55 us -> 49 us  [shards(): pl.pallas_call(functools.partial(kernel, zs, xs), out_shape=(pltpu.VMEM(p...]
where the time goes in v3:
time: 51.1 us; the launch traced here: 51 us
  Pallas kernels  49 us (96%)
  local copies, waits for them, and re-layouts  1.3 us (3%)
  between operations  0.64 us (1%)
    pallas_call x1, Pallas kernels, shards(): pl.pallas_call(functools.partial(kernel, zs, xs), out_shape=(pltpu.VMEM(p...  49 us
    unnamed x2, local copies, waits for them, and re-layouts  1.3 us

profile of v3, /device:TPU:1, one launch (start us, length us, event | category | flops | bytes accessed | tf_op | source)
XLA Modules:
  0.0 51.0 jit_solution(11843907032338160206)
XLA Ops:
  0.6 49.0 %shard_map.122 = (f32[8,64,128]{2,1,0:T(8,128)S(1)}, f32[8,128]{1,0:T(8,128)S(1)}) custom-call(f32[8,64,128]{2,1,0:T(8,128)} %pops.1, f32[64,128]{1,0:T(8,128)} %bitcast.3, f32[64,128]{1,0:T(8,128)} %sto.1, s32[2,128,8,128]{3,2,1,0:T(8,128)} %draws.1, f32[8]{0:T(128)} %rates.1, s32[4,64]{1,0:T(4,128)} %bitcast.5, s32[2,4,64]{2,1,0:T(4,128)} %bitcast.4, ...), custom_call_target="tpu_custom_call" | custom-call | tf_op jit(solution)/shard_map/pallas_call | solution.py:425
  49.7 0.7 %copy.15 = f32[8,64,128]{2,1,0:T(8,128)} copy(f32[8,64,128]{2,1,0:T(8,128)S(1)} %get-tuple-element.2) | data formatting | bytes 524288
  50.4 0.6 %copy.16 = f32[8,128]{1,0:T(8,128)} copy(f32[8,128]{1,0:T(8,128)S(1)} %get-tuple-element.3) | data formatting | bytes 8192

commit v4 on v3

--- a/solution.py
+++ b/solution.py
@@ -12,7 +12,8 @@
 BF16 = jnp.bfloat16
 
 PARTNERS = ((1, 0), (3, 0), (1, 1), (3, 1), (2, 0), (2, 1), (0, 1))
-DIRECT = ((0, 1), (1, 0), (3, 0), (1, 1), (3, 1))
+FARTHEST = ((2, 1), (2, 0), (1, 1), (3, 1), (1, 0), (3, 0), (0, 1))
+DIRECT = (((0, 1), (1, 0), (3, 1)), ((0, 1), (1, 0), (3, 0), (1, 1), (3, 1)))
 SHIFT = 4.0
 VLIM = 62
 HALF = (4, 8)
@@ -215,7 +216,7 @@
         for i, rel in enumerate(PARTNERS):
             m = peer(rel)
             send(reacted(m), chunk(k, 1, n, h), sh.at[k], r2.at[k, h, i], (w, m))
-        for rel in ((0, 0),) + DIRECT:
+        for rel in ((0, 0),) + DIRECT[k]:
             m = peer(rel)
             slot = 7 if rel == (0, 0) else PARTNERS.index(rel)
             send(reacted(m), chunk(k, 2, n, h), sh.at[k], rh.at[k, h, 1, slot], (left, m))
@@ -226,7 +227,7 @@
 
     def forward_reacted(k, h):
         for i, rel in enumerate(PARTNERS):
-            if rel in DIRECT:
+            if rel in DIRECT[k]:
                 continue
             m = source(rel)
             wait(chunk(k, 1, m, h), r2.at[k, h, i])
@@ -235,7 +236,7 @@
 
     def wait_reacted(k, h):
         for i, rel in enumerate(PARTNERS):
-            if rel in DIRECT:
+            if rel in DIRECT[k]:
                 wait(chunk(k, 1, source(rel), h), r2.at[k, h, i])
         for i, rel in enumerate(PARTNERS + ((0, 0),)):
             for side in (0, 1):
@@ -266,9 +267,9 @@
     for h in range(8 // HALF[0]):
         send_reacted(0, h)
     keep_reacted(0)
+    forward_reacted(0, 0)
     hop_tables()
-    for h in range(8 // HALF[0]):
-        forward_reacted(0, h)
+    forward_reacted(0, 1)
     pl.semaphore_wait(near.at[1], 2)
     reach(2)
     lax.fori_loop(0, 24, tables, 0)
@@ -301,10 +302,10 @@
         v = v + ep[1, s // 8, s % 8 : s % 8 + 1, :] * tile
     uv[2, eight(n)] = v
     uv[3, eight(n)] = u
-    for rel in PARTNERS + ((0, 0),):
+    for rel in FARTHEST + ((0, 0),):
         send(uv.at[2, eight(n)], uv.at[1, eight(n)], su.at[1], ru.at[1], (left, peer(rel)))
         send(uv.at[2, eight(n)], uv.at[0, eight(n)], su.at[1], ru.at[1], (right, peer(rel)))
-    for rel in PARTNERS:
+    for rel in FARTHEST:
         mine = uv.at[2:4, eight(n), :]
         send(mine, mine, su.at[0], ru.at[0], (w, peer(rel)))
     send_reacted(1, 0)

time: 51.1 us -> 50.2 us (0.982)
  Pallas kernels: 49 us -> 47.8 us
    pallas_call x1, Pallas kernels: 49 us -> 47.8 us  [shards(): pl.pallas_call(functools.partial(kernel, zs, xs), out_shape=(pltpu.VMEM(p...]
where the time goes in v4:
time: 50.2 us; the launch traced here: 49.7 us
  Pallas kernels  47.8 us (95%)
  local copies, waits for them, and re-layouts  1.3 us (3%)
  between operations  0.64 us (1%)
    pallas_call x1, Pallas kernels, shards(): pl.pallas_call(functools.partial(kernel, zs, xs), out_shape=(pltpu.VMEM(p...  47.8 us
    unnamed x2, local copies, waits for them, and re-layouts  1.3 us

profile of v4, /device:TPU:1, one launch (start us, length us, event | category | flops | bytes accessed | tf_op | source)
XLA Modules:
  0.0 49.7 jit_solution(14341613395564254346)
XLA Ops:
  0.6 47.8 %shard_map.122 = (f32[8,64,128]{2,1,0:T(8,128)S(1)}, f32[8,128]{1,0:T(8,128)S(1)}) custom-call(f32[8,64,128]{2,1,0:T(8,128)} %pops.1, f32[64,128]{1,0:T(8,128)} %bitcast.3, f32[64,128]{1,0:T(8,128)} %sto.1, s32[2,128,8,128]{3,2,1,0:T(8,128)} %draws.1, f32[8]{0:T(128)} %rates.1, s32[4,64]{1,0:T(4,128)} %bitcast.5, s32[2,4,64]{2,1,0:T(4,128)} %bitcast.4, ...), custom_call_target="tpu_custom_call" | custom-call | tf_op jit(solution)/shard_map/pallas_call | solution.py:426
  48.4 0.7 %copy.15 = f32[8,64,128]{2,1,0:T(8,128)} copy(f32[8,64,128]{2,1,0:T(8,128)S(1)} %get-tuple-element.2) | data formatting | bytes 524288
  49.1 0.6 %copy.16 = f32[8,128]{1,0:T(8,128)} copy(f32[8,128]{1,0:T(8,128)S(1)} %get-tuple-element.3) | data formatting | bytes 8192

commit v5 on v4

--- a/solution.py
+++ b/solution.py
@@ -16,7 +16,7 @@
 DIRECT = (((0, 1), (1, 0), (3, 1)), ((0, 1), (1, 0), (3, 0), (1, 1), (3, 1)))
 SHIFT = 4.0
 VLIM = 62
-HALF = (4, 8)
+HALF = (2, 8)
 
 
 def split(x):
@@ -268,8 +268,10 @@
         send_reacted(0, h)
     keep_reacted(0)
     forward_reacted(0, 0)
+    forward_reacted(0, 1)
     hop_tables()
-    forward_reacted(0, 1)
+    forward_reacted(0, 2)
+    forward_reacted(0, 3)
     pl.semaphore_wait(near.at[1], 2)
     reach(2)
     lax.fori_loop(0, 24, tables, 0)
@@ -391,14 +393,6 @@
     amounts = pltpu.make_async_copy(diff.at[1], out_pops, loc.at[10])
     amounts.start()
 
-    wait(mz.at[0 : wides - 1], so.at[1])
-    tile = jnp.sum(mz[...].reshape(wides, 128), axis=0, keepdims=True)
-    sums = jnp.sum(jnp.where(diagonal, tile, 0.0), axis=1, keepdims=True)
-    a, b, c = krylov_coefficients([sums[k : k + 1] for k in range(6)])
-    msf_v[...] = a * fields[0, n] + b * fields[1, n] + c * fields[2, n]
-    voltage = pltpu.make_async_copy(msf_v, out_pot, loc.at[11])
-    voltage.start()
-
     for k in range(2):
         wait(gath.at[k, 0:56], sa.at[k])
         wait(halo.at[k, 0:23], sh.at[k])
@@ -409,9 +403,14 @@
     wait(uv.at[0:2], su.at[1])
     wait(edge.at[0], sg.at[0])
     wait(edge.at[1], sg.at[1])
+    wait(mz.at[0 : wides - 1], so.at[1])
+    tile = jnp.sum(mz[...].reshape(wides, 128), axis=0, keepdims=True)
+    sums = jnp.sum(jnp.where(diagonal, tile, 0.0), axis=1, keepdims=True)
+    a, b, c = krylov_coefficients([sums[k : k + 1] for k in range(6)])
+    out_pot[...] = a * fields[0, n] + b * fields[1, n] + c * fields[2, n]
+
     wait(mz.at[0 : wides - 1], so.at[0])
     amounts.wait()
-    voltage.wait()
 
 
 def solution(mesh):
@@ -430,7 +429,7 @@
                 pltpu.VMEM(msf.shape, F32),
             ),
             in_specs=[hbm_spec] * 11,
-            out_specs=(any_spec, any_spec),
+            out_specs=(any_spec, pl.BlockSpec(memory_space=pltpu.VMEM)),
             scratch_shapes=[
                 vmem((2, 64, 8, 128), F32),
                 vmem((2, 64, 8, 128), F32),

time: 50.2 us -> 50.1 us (level)
  no operation moved by 1% of the time
where the time goes in v5:
time: 50.1 us; the launch traced here: 49.9 us
  Pallas kernels  47.9 us (96%)
  local copies, waits for them, and re-layouts  1.3 us (3%)
  between operations  0.64 us (1%)
    pallas_call x1, Pallas kernels, shards(): pl.pallas_call(functools.partial(kernel, zs, xs), out_shape=(pltpu.VMEM(p...  47.9 us
    unnamed x2, local copies, waits for them, and re-layouts  1.3 us

profile of v5, /device:TPU:1, one launch (start us, length us, event | category | flops | bytes accessed | tf_op | source)
XLA Modules:
  0.0 49.9 jit_solution(825642258517806020)
XLA Ops:
  0.6 47.9 %shard_map.122 = (f32[8,64,128]{2,1,0:T(8,128)S(1)}, f32[8,128]{1,0:T(8,128)S(1)}) custom-call(f32[8,64,128]{2,1,0:T(8,128)} %pops.1, f32[64,128]{1,0:T(8,128)} %bitcast.3, f32[64,128]{1,0:T(8,128)} %sto.1, s32[2,128,8,128]{3,2,1,0:T(8,128)} %draws.1, f32[8]{0:T(128)} %rates.1, s32[4,64]{1,0:T(4,128)} %bitcast.5, s32[2,4,64]{2,1,0:T(4,128)} %bitcast.4, ...), custom_call_target="tpu_custom_call" | custom-call | tf_op jit(solution)/shard_map/pallas_call | solution.py:425
  48.6 0.7 %copy.15 = f32[8,64,128]{2,1,0:T(8,128)} copy(f32[8,64,128]{2,1,0:T(8,128)S(1)} %get-tuple-element.2) | data formatting | bytes 524288
  49.3 0.6 %copy.16 = f32[8,128]{1,0:T(8,128)} copy(f32[8,128]{1,0:T(8,128)S(1)} %get-tuple-element.3) | data formatting | bytes 8192
